TPU v7x, 128 devices: a whole 4x4x4 slice. The times are simulated.
128 devices in a mesh: gx: 8 (over x, core), gy: 16 (over z, y).
Axes of the slice: x: 4, y: 4, z: 4, core: 2. Of those that a mesh axis runs over, the one named last changes fastest.
Arguments:
- vectors: float32 [4, 262144], P(None, ('gx', 'gy')), may hold values from -6 to 6
- cluster_order: int32 [128, 2048], P(('gx', 'gy')), may hold values from 0 to 2047, each once within a row
- near_blocks: float32 [32, 64, 128, 9, 128], P('gx', 'gy'), may hold values from -0.1875 to 0.1875
- leaf_basis: float32 [32, 64, 128, 64], P('gx', 'gy'), may hold values from -0.5 to 0.5
- couple_leaf: float32 [32, 64, 64, 27, 64], P('gx', 'gy'), may hold values from -0.15625 to 0.15625
- transfer_leaf: float32 [32, 64, 64, 64], P('gx', 'gy'), may hold values from -0.5 to 0.5
- couple_node: float32 [16, 32, 64, 27, 64], P('gx', 'gy'), may hold values from -0.15625 to 0.15625
- transfer_node: float32 [16, 32, 64, 64], P('gx', 'gy'), may hold values from -0.5 to 0.5
- transfer_device: float32 [8, 16, 64, 64], P('gx', 'gy'), may hold values from -0.5 to 0.5
- couple_upper: float32 [128, 35, 64, 64], P(('gx', 'gy')), may hold values from -0.15625 to 0.15625
- pair_list: int32 [2, 128, 35], P(None, ('gx', 'gy')), may hold values from 0 to 160
Outputs:
- product: float32 [4, 262144], P(None, ('gx', 'gy'))
Inputs may be any that keep to these rules, and one draw needn't show every extreme that they name: Every admissible pair appears in exactly one slot: device boxes whose parents are equal or adjacent (also diagonally) but which are not themselves adjacent, and level 3 boxes that are not adjacent. A slot with target 160 is empty and has source 0.
All inputs are finite; a program needn't handle non-finite values.
Results may differ from a plain program's by a relative error of at most 0.000054.
Values sent between devices are 32-bit elements; how exact they have to be, the bound alone decides.
A program may use at most 128 MiB of HBM per device.

v0:
```python
import functools

import jax
import jax.numpy as jnp
from jax import lax
from jax.experimental import pallas as pl
from jax.experimental.pallas import tpu as pltpu
from jax.sharding import PartitionSpec as P

F32 = jnp.float32
BF16 = jnp.bfloat16
MESH = pl.DeviceIdType.MESH
NT = (((1,), (1,)), ((), ()))
NN = (((1,), (0,)), ((), ()))
DIRECTIONS = [(dx, dy) for dx in (-1, 0, 1) for dy in (-1, 0, 1) if (dx, dy) != (0, 0)]


def slots_of(s, w):
    return [
        (i, j)
        for i in range(6)
        for j in range(6)
        if not (s + 1 <= i <= s + 3 and w + 1 <= j <= w + 3)
    ]


def high_low(values):
    high = values.astype(BF16)
    return high, (values - high.astype(F32)).astype(BF16)


def stack_split(rows):
    high = rows.astype(BF16).astype(F32)
    return jnp.concatenate([high, rows - high], 0).astype(BF16)


def split_dot(stacked, matrix, dims):
    high, low = high_low(matrix)
    return lax.dot_general(stacked, high, dims, preferred_element_type=F32) + lax.dot_general(
        stacked, low, dims, preferred_element_type=F32
    )


def fold(rows):
    return rows[0:4] + rows[4:8]


def kernel(
    n_x, n_y, slots,
    vec_h, ord_h, near_h, bas_h, cl_h, tl_h, cn_h, tn_h, td_h, cu_h, pairs_h, pairs_s,
    out_ref,
    vec_v, ord_v, near_v, bas_v, cl_v, tl_v, cn_v, tn_v, td_v, cu_v, pairs_v,
    vs_v, onehot_v, ext, xs_v, nodex, table, tbl2, prod, rs_send, rs_recv, rs1, rs2,
    far_node, far_leaf, near_y, y_v,
    small_sem, near_sem, cl_sem, cn_sem,
    halo_send, halo_recv, ag1_send, ag1_recv, ag2_send, ag2_recv,
    rsa_send, rsa_recv, rsb_send, rsb_recv,
):
    gi, gj = lax.axis_index("gx"), lax.axis_index("gy")

    small = [
        pltpu.make_async_copy(src, dst, small_sem.at[k])
        for k, (src, dst) in enumerate([
            (vec_h, vec_v), (ord_h, ord_v), (bas_h, bas_v), (tl_h, tl_v), (tn_h, tn_v),
            (td_h, td_v), (pairs_h, pairs_v), (cu_h, cu_v),
        ])
    ]
    for copy in small:
        copy.start()
    node_copy = pltpu.make_async_copy(cn_h, cn_v, cn_sem)
    node_copy.start()

    def cl_copy(leaf):
        return pltpu.make_async_copy(cl_h.at[leaf], cl_v.at[leaf], cl_sem.at[leaf])

    def near_copy(leaf):
        return pltpu.make_async_copy(near_h.at[leaf], near_v.at[leaf], near_sem.at[leaf])

    for u in range(2):
        for v in range(2):
            for s in range(2):
                for w in range(2):
                    cl_copy((2 * u + s) * 4 + 2 * v + w).start()
    for leaf in range(16):
        near_copy(leaf).start()

    ext[...] = jnp.zeros_like(ext)

    def inside(dx, dy):
        ok = None
        for pos, step, count in ((gi, dx, n_x), (gj, dy, n_y)):
            if step == 0:
                continue
            here = pos + step < count if step > 0 else pos + step >= 0
            ok = here if ok is None else jnp.logical_and(ok, here)
        return ok

    barrier = pltpu.get_barrier_semaphore()
    for k in range(1, n_x):
        pl.semaphore_signal(barrier, inc=1, device_id=(lax.rem(gi + k, n_x), gj), device_id_type=MESH)
    for k in range(1, n_y):
        pl.semaphore_signal(barrier, inc=1, device_id=(gi, lax.rem(gj + k, n_y)), device_id_type=MESH)
    diagonal = 0
    for dx, dy in DIRECTIONS:
        if dx != 0 and dy != 0:
            ok = inside(dx, dy)
            diagonal = diagonal + ok.astype(jnp.int32)

            @pl.when(ok)
            def _(dx=dx, dy=dy):
                pl.semaphore_signal(barrier, inc=1, device_id=(gi + dx, gj + dy), device_id_type=MESH)

    small[0].wait()
    small[1].wait()
    vec = vec_v[...]
    vec_high = vec.astype(BF16).astype(F32)
    vec_low = vec - vec_high
    for kh in range(16):
        cols = slice(kh * 128, kh * 128 + 128)
        vs_v[kh * 8 : kh * 8 + 4, :] = vec_high[:, cols]
        vs_v[kh * 8 + 4 : kh * 8 + 8, :] = vec_low[:, cols]
    order = ord_v[...]
    order_low = jnp.bitwise_and(order, 127)
    order_high = lax.shift_right_logical(order, 7)
    sub = lax.broadcasted_iota(jnp.int32, (128, 128), 0)
    row_group = lax.shift_right_logical(sub, 3)
    vs = vs_v[...].astype(BF16)
    small[2].wait()
    for leaf in range(16):
        cols = slice(leaf * 128, leaf * 128 + 128)
        onehot = jnp.where(sub == order_low[:, cols], 1.0, 0.0).astype(BF16)
        onehot_v[:, cols] = onehot
        picked = lax.dot_general(vs, onehot, NN, preferred_element_type=F32)
        picked = jnp.where(row_group == order_high[:, cols], picked, 0.0)
        stacked = jnp.sum(picked.reshape(16, 8, 128), axis=0)
        up = fold(split_dot(stacked.astype(BF16), bas_v[leaf], NT))
        a, b = leaf // 4, leaf % 4
        ext[2 + a, 2 + b, 0:4, :] = fold(stacked)
        ext[2 + a, 2 + b, 4:8, 0:64] = up

    small[3].wait()
    small[4].wait()
    small[5].wait()
    up_device = jnp.zeros((8, 64), F32)
    for u in range(2):
        for v in range(2):
            node = jnp.zeros((8, 64), F32)
            for s in range(2):
                for w in range(2):
                    a, b = 2 * u + s, 2 * v + w
                    child = stack_split(ext[2 + a, 2 + b, 4:8, 0:64])
                    node = node + split_dot(child, tl_v[a * 4 + b], NN)
            node = fold(node)
            for p in range(2):
                for q in range(2):
                    ext[2 + 2 * p + u, 2 + 2 * q + v, 4:8, 64:128] = node
            up_device = up_device + split_dot(stack_split(node), tn_v[u * 2 + v], NN)
    up_device = fold(up_device)
    toward = fold(split_dot(stack_split(up_device), td_v[...], NN))
    table[gj, gi] = jnp.concatenate([up_device, toward], 1)

    pl.semaphore_wait(barrier, n_x - 1 + n_y - 1 + diagonal)

    def ag1(to):
        return pltpu.make_async_remote_copy(
            src_ref=table.at[gj, gi], dst_ref=table.at[gj, gi],
            send_sem=ag1_send.at[to], recv_sem=ag1_recv.at[gi],
            device_id=(to, gj), device_id_type=MESH)

    def ag1_in(source):
        return pltpu.make_async_remote_copy(
            src_ref=table.at[gj, gi], dst_ref=table.at[gj, source],
            send_sem=ag1_send.at[source], recv_sem=ag1_recv.at[source],
            device_id=(source, gj), device_id_type=MESH)

    for k in range(1, n_x):
        ag1(lax.rem(gi + k, n_x)).start()

    cut = {-1: (2, 2, 6), 0: (2, 4, 2), 1: (4, 2, 0)}

    def halo(index):
        dx, dy = DIRECTIONS[index]
        (r0, rn, rd), (c0, cn, cd) = cut[dx], cut[dy]
        return pltpu.make_async_remote_copy(
            src_ref=ext.at[r0 : r0 + rn, c0 : c0 + cn], dst_ref=ext.at[rd : rd + rn, cd : cd + cn],
            send_sem=halo_send.at[index], recv_sem=halo_recv.at[index],
            device_id=(gi + dx, gj + dy), device_id_type=MESH)

    for index, (dx, dy) in enumerate(DIRECTIONS):
        @pl.when(inside(dx, dy))
        def _(index=index):
            halo(index).start()

    for k in range(1, n_x):
        ag1_in(lax.rem(gi + k, n_x)).wait_recv()

    def ag2(to):
        return pltpu.make_async_remote_copy(
            src_ref=table.at[gj], dst_ref=table.at[gj],
            send_sem=ag2_send.at[to], recv_sem=ag2_recv.at[gj],
            device_id=(gi, to), device_id_type=MESH)

    def ag2_in(source):
        return pltpu.make_async_remote_copy(
            src_ref=table.at[gj], dst_ref=table.at[source],
            send_sem=ag2_send.at[source], recv_sem=ag2_recv.at[source],
            device_id=(gi, source), device_id_type=MESH)

    for k in range(1, n_y):
        ag2(lax.rem(gj + k, n_y)).start()

    for index, (dx, dy) in enumerate(DIRECTIONS):
        @pl.when(inside(dx, dy))
        def _(dx=dx, dy=dy):
            halo(DIRECTIONS.index((-dx, -dy))).wait_recv()

    for r in range(6):
        for c in range(6):
            x = ext[r + 1, c + 1, 0:4, :]
            high = x.astype(BF16).astype(F32)
            xs_v[r, c, 0:4, :] = high
            xs_v[r, c, 4:8, :] = x - high
            tile_r, tile_c = (0, 2, 6)[r // 2] + r % 2, (0, 2, 6)[c // 2] + c % 2
            nodex[r, c, 0:4, :] = pltpu.roll(ext[tile_r, tile_c], 64, 1)[4:8]

    row8 = lax.broadcasted_iota(jnp.int32, (8, 64), 0)
    pick_row = [jnp.where(row8 == n, 1.0, 0.0).astype(BF16) for n in range(4)]

    def far_sum(blocks, source):
        acc = [jnp.zeros((64, 64), F32) for _ in range(4)]
        for g in range(27):
            block = blocks(g)
            for n in range(4):
                acc[n] = acc[n] + block * source(g, n)
        total = jnp.zeros((8, 64), F32)
        for n in range(4):
            for part in high_low(acc[n]):
                total = total + lax.dot_general(pick_row[n], part, NT, preferred_element_type=F32)
        return total

    def far_leaf_group(u, v):
        for s in range(2):
            for w in range(2):
                layout = slots_of(s, w)
                leaf = (2 * u + s) * 4 + 2 * v + w
                cl_copy(leaf).wait()
                far_leaf[leaf] = far_sum(
                    lambda g: cl_v[leaf, g],
                    lambda g, n: ext[2 * u + layout[g][0], 2 * v + layout[g][1], 4 + n : 5 + n, 0:64],
                )

    def far_node_group(box, s, w):
        layout = slots_of(s, w)
        far_node[box] = far_sum(
            lambda g: cn_v[box, g],
            lambda g, n: nodex[layout[g][0], layout[g][1], n : n + 1, 0:64],
        )

    def near_leaf(leaf):
        a, b = lax.div(leaf, 4), lax.rem(leaf, 4)
        near_copy(leaf).wait()
        total = jnp.zeros((8, 128), F32)
        for e in range(9):
            stacked = xs_v[a + e // 3, b + e % 3].astype(BF16)
            total = total + split_dot(stacked, near_v[leaf, e], NT)
        near_y[leaf] = total

    def loop(low, high, body):
        lax.fori_loop(low, high, lambda k, c: (body(k), c)[1], 0)

    node_copy.wait()
    for s in range(2):
        for w in range(2):
            far_node_group(2 * s + w, s, w)
    loop(0, 2, lambda v: far_leaf_group(0, v))

    for k in range(1, n_y):
        ag2_in(lax.rem(gj + k, n_y)).wait_recv()

    devices = n_x * n_y
    full = table[...]
    groups = full.reshape(n_y // 2, 2, n_x // 2, 2, 4, 128).sum(axis=(1, 3)).reshape(devices // 4, 4, 128)
    full = full.reshape(devices, 4, 128)
    high = full.astype(BF16).astype(F32)
    tbl2[0:devices, 0:4, :] = high
    tbl2[0:devices, 4:8, :] = full - high
    high = groups.astype(BF16).astype(F32)
    tbl2[devices:, 0:4, :] = pltpu.roll(high, 64, 2)
    tbl2[devices:, 4:8, :] = pltpu.roll(groups - high, 64, 2)

    small[6].wait()
    small[7].wait()
    prod[...] = jnp.zeros_like(prod)
    for k in range(slots):
        source = pairs_s[1, 0, k]
        group = source - devices
        place = jnp.where(
            source < devices,
            lax.rem(source, n_y) * n_x + lax.div(source, n_y),
            devices + lax.rem(group, n_y // 2) * (n_x // 2) + lax.div(group, n_y // 2),
        )
        stacked = tbl2[place, :, 0:64].astype(BF16)
        prod[k * 8 : k * 8 + 4, 0:64] = fold(split_dot(stacked, cu_v[k], NT))

    target = pairs_v[0]
    row = lax.broadcasted_iota(jnp.int32, (devices, slots), 0)
    row_j, row_i = lax.div(row, n_x), lax.rem(row, n_x)
    own_box = row_i * n_y + row_j
    parent_box = devices + lax.div(row_i, 2) * (n_y // 2) + lax.div(row_j, 2)
    pick_own = jnp.where(own_box == target, 1.0, 0.0).astype(BF16)
    pick_parent = jnp.where(parent_box == target, 1.0, 0.0).astype(BF16)
    for n in range(4):
        rows = prod[pl.ds(n, 40, stride=8), :][0:slots, 0:64]
        sums = []
        for pick in (pick_own, pick_parent):
            part = 0.0
            for piece in high_low(rows):
                part = part + lax.dot_general(pick, piece, NN, preferred_element_type=F32)
            sums.append(part)
        both = jnp.concatenate(sums, 1)
        rs_send[:, :, n : n + 1, :] = both.reshape(n_y, n_x, 1, 128)

    def rsa(to):
        return pltpu.make_async_remote_copy(
            src_ref=rs_send.at[to], dst_ref=rs_recv.at[gj],
            send_sem=rsa_send.at[to], recv_sem=rsa_recv.at[gj],
            device_id=(gi, to), device_id_type=MESH)

    def rsa_in(source):
        return pltpu.make_async_remote_copy(
            src_ref=rs_send.at[source], dst_ref=rs_recv.at[source],
            send_sem=rsa_send.at[source], recv_sem=rsa_recv.at[source],
            device_id=(gi, source), device_id_type=MESH)

    for k in range(1, n_y):
        rsa(lax.rem(gj + k, n_y)).start()
    rs_recv[gj] = rs_send[gj]

    loop(0, 2, lambda v: far_leaf_group(1, v))
    loop(0, 4, near_leaf)

    for k in range(1, n_y):
        rsa_in(lax.rem(gj + k, n_y)).wait_recv()
    rs1[...] = jnp.sum(rs_recv[...], axis=0)

    def rsb(to):
        return pltpu.make_async_remote_copy(
            src_ref=rs1.at[to], dst_ref=rs2.at[gi],
            send_sem=rsb_send.at[to], recv_sem=rsb_recv.at[gi],
            device_id=(to, gj), device_id_type=MESH)

    def rsb_in(source):
        return pltpu.make_async_remote_copy(
            src_ref=rs1.at[source], dst_ref=rs2.at[source],
            send_sem=rsb_send.at[source], recv_sem=rsb_recv.at[source],
            device_id=(source, gj), device_id_type=MESH)

    for k in range(1, n_x):
        rsb(lax.rem(gi + k, n_x)).start()
    rs2[gi] = rs1[gi]

    loop(4, 16, near_leaf)

    for k in range(1, n_x):
        rsb_in(lax.rem(gi + k, n_x)).wait_recv()
    sums = jnp.sum(rs2[...], axis=0)

    down_device = sums[:, 0:64] + fold(split_dot(stack_split(sums[:, 64:128]), td_v[...], NT))
    device_rows = stack_split(down_device)
    for u in range(2):
        for v in range(2):
            box = u * 2 + v
            down_node = far_node[box][0:4] + fold(split_dot(device_rows, tn_v[box], NT))
            node_rows = stack_split(down_node)
            for s in range(2):
                for w in range(2):
                    leaf = (2 * u + s) * 4 + 2 * v + w
                    down_leaf = far_leaf[leaf][0:4] + fold(split_dot(node_rows, tl_v[leaf], NT))
                    y = split_dot(stack_split(down_leaf), bas_v[leaf], NN) + near_y[leaf]
                    y_v[:, leaf * 128 : leaf * 128 + 128] = stack_split(fold(y)).astype(F32)

    total = jnp.zeros((128, 128), F32)
    for leaf in range(16):
        cols = slice(leaf * 128, leaf * 128 + 128)
        y = y_v[:, cols]
        spread = jnp.broadcast_to(y[None], (16, 8, 128)).reshape(128, 128)
        spread = jnp.where(row_group == order_high[:, cols], spread, 0.0).astype(BF16)
        total = total + lax.dot_general(spread, onehot_v[:, cols], NT, preferred_element_type=F32)
    for kh in range(16):
        out_ref[:, kh * 128 : kh * 128 + 128] = fold(total[kh * 8 : kh * 8 + 8])

    for k in range(1, n_x):
        ag1(lax.rem(gi + k, n_x)).wait_send()
        rsb(lax.rem(gi + k, n_x)).wait_send()
    for k in range(1, n_y):
        ag2(lax.rem(gj + k, n_y)).wait_send()
        rsa(lax.rem(gj + k, n_y)).wait_send()
    for index, (dx, dy) in enumerate(DIRECTIONS):
        @pl.when(inside(dx, dy))
        def _(index=index):
            halo(index).wait_send()


def on_device(
    n_x, n_y,
    vectors, cluster_order, near_blocks, leaf_basis, couple_leaf, transfer_leaf,
    couple_node, transfer_node, transfer_device, couple_upper, pair_list,
):
    slots = couple_upper.shape[1]
    devices = n_x * n_y
    near = near_blocks.transpose(0, 1, 3, 2, 4).reshape(16, 9, 128, 128)
    basis = leaf_basis.transpose(0, 1, 3, 2).reshape(16, 64, 128)
    cl = couple_leaf.transpose(0, 1, 3, 2, 4).reshape(16, 27, 64, 64)
    cn = couple_node.transpose(0, 1, 3, 2, 4).reshape(4, 27, 64, 64)
    tl = transfer_leaf.reshape(16, 64, 64)
    tn = transfer_node.reshape(4, 64, 64)
    td = transfer_device.reshape(64, 64)
    cu = couple_upper.reshape(slots, 64, 64)
    dma = pltpu.SemaphoreType.DMA
    any_spec = pl.BlockSpec(memory_space=pl.ANY)
    return pl.pallas_call(
        functools.partial(kernel, n_x, n_y, slots),
        out_shape=jax.ShapeDtypeStruct((4, 2048), F32),
        in_specs=[any_spec] * 11 + [pl.BlockSpec(memory_space=pltpu.SMEM)],
        out_specs=pl.BlockSpec(memory_space=pltpu.VMEM),
        scratch_shapes=[
            pltpu.VMEM((4, 2048), F32),
            pltpu.VMEM((1, 2048), jnp.int32),
            pltpu.VMEM((16, 9, 128, 128), F32),
            pltpu.VMEM((16, 64, 128), F32),
            pltpu.VMEM((16, 27, 64, 64), F32),
            pltpu.VMEM((16, 64, 64), F32),
            pltpu.VMEM((4, 27, 64, 64), F32),
            pltpu.VMEM((4, 64, 64), F32),
            pltpu.VMEM((64, 64), F32),
            pltpu.VMEM((slots, 64, 64), F32),
            pltpu.VMEM((2, 1, slots), jnp.int32),
            pltpu.VMEM((128, 128), F32),
            pltpu.VMEM((128, 2048), BF16),
            pltpu.VMEM((8, 8, 8, 128), F32),
            pltpu.VMEM((6, 6, 8, 128), F32),
            pltpu.VMEM((6, 6, 8, 128), F32),
            pltpu.VMEM((n_y, n_x, 4, 128), F32),
            pltpu.VMEM((devices + devices // 4, 8, 128), F32),
            pltpu.VMEM((320, 128), F32),
            pltpu.VMEM((n_y, n_x, 4, 128), F32),
            pltpu.VMEM((n_y, n_x, 4, 128), F32),
            pltpu.VMEM((n_x, 4, 128), F32),
            pltpu.VMEM((n_x, 4, 128), F32),
            pltpu.VMEM((4, 8, 64), F32),
            pltpu.VMEM((16, 8, 64), F32),
            pltpu.VMEM((16, 8, 128), F32),
            pltpu.VMEM((8, 2048), F32),
            dma((8,)), dma((16,)), dma((16,)), dma(()),
            dma((8,)), dma((8,)), dma((n_x,)), dma((n_x,)), dma((n_y,)), dma((n_y,)),
            dma((n_y,)), dma((n_y,)), dma((n_x,)), dma((n_x,)),
        ],
        compiler_params=pltpu.CompilerParams(
            collective_id=0, has_side_effects=True, vmem_limit_bytes=56 * 1024 * 1024
        ),
    )(vectors, cluster_order, near, basis, cl, tl, cn, tn, td, cu, pair_list, pair_list)


def solution(mesh):
    in_specs = (
        P(None, ("gx", "gy")),
        P(("gx", "gy"), None),
        P("gx", "gy", None, None, None),
        P("gx", "gy", None, None),
        P("gx", "gy", None, None, None),
        P("gx", "gy", None, None),
        P("gx", "gy", None, None, None),
        P("gx", "gy", None, None),
        P("gx", "gy", None, None),
        P(("gx", "gy"), None, None, None),
        P(None, ("gx", "gy"), None),
    )
    out_specs = P(None, ("gx", "gy"))
    return jax.shard_map(
        functools.partial(on_device, mesh.shape["gx"], mesh.shape["gy"]),
        mesh=mesh, in_specs=in_specs, out_specs=out_specs, check_vma=False,
    )
```

profile of v0, /device:TPU:1, one launch (start us, length us, event | category | flops | bytes accessed | tf_op | source)
XLA Modules:
  0.0 41.3 jit_solution(13384070254921043382)
XLA Ops:
  0.0 39.9 %shard_map.109 = f32[4,2048]{1,0:T(4,128)} custom-call(f32[4,2048]{1,0:T(4,128)} %vec_h.1, s32[1,2048]{1,0:T(1,128)} %ord_h.1, f32[16,9,128,128]{3,2,1,0:T(8,128)} %bitcast.17, f32[16,64,128]{2,1,0:T(8,128)} %bitcast.20, f32[16,27,64,64]{3,2,1,0:T(8,128)} %bitcast.16, f32[16,64,64]{2,1,0:T(8,128)} %bitcast.21, f32[4,27,64,64]{3,2,1,0:T(8,128)} %bitcast.18, ...), custom_call_target="tpu_custom_call" | custom-call | tf_op jit(solution)/shard_map/pallas_call | solution.py:421
  39.9 1.4 %copy.13 = f32[4,2048]{1,0:T(4,128)} copy(f32[4,2048]{1,0:T(4,128)} %shard_map.109) | data formatting | bytes 65536
where the time goes:
time: 41.7 us; the launch traced here: 41.3 us
  Pallas kernels  39.9 us (96%)
  local copies, waits for them, and re-layouts  1.38 us (3%)
    pallas_call x1, Pallas kernels, on_device(): pl.pallas_call(functools.partial(kernel, n_x, n_y, slots), out_shape=jax....  39.9 us
    unnamed x1, local copies, waits for them, and re-layouts  1.38 us

commit v1 on v0

v1 whole, which is shorter than its diff:
```python
import functools

import jax
import jax.numpy as jnp
from jax import lax
from jax.experimental import pallas as pl
from jax.experimental.pallas import tpu as pltpu
from jax.sharding import PartitionSpec as P

F32 = jnp.float32
BF16 = jnp.bfloat16
MESH = pl.DeviceIdType.MESH
NT = (((1,), (1,)), ((), ()))
NN = (((1,), (0,)), ((), ()))
TN = (((0,), (0,)), ((), ()))
DIRECTIONS = [(dx, dy) for dx in (-1, 0, 1) for dy in (-1, 0, 1) if (dx, dy) != (0, 0)]


HOPS = (0, 1, 2, 1)
OFFSETS = sorted(
    [
        (x, y, z, c)
        for c in range(2)
        for x in range(4)
        for y in range(4)
        for z in range(4)
        if (x, y, z, c) != (0, 0, 0, 0)
    ],
    key=lambda o: -(HOPS[o[0]] + HOPS[o[1]] + HOPS[o[2]]),
)


def slots_of(s, w):
    return [
        (i, j)
        for i in range(6)
        for j in range(6)
        if not (s + 1 <= i <= s + 3 and w + 1 <= j <= w + 3)
    ]


def high_low(values):
    high = values.astype(BF16)
    return high, (values - high.astype(F32)).astype(BF16)


def stack_split(rows):
    high = rows.astype(BF16).astype(F32)
    return jnp.concatenate([high, rows - high], 0).astype(BF16)


def split_dot(stacked, matrix, dims):
    high, low = high_low(matrix)
    return lax.dot_general(stacked, high, dims, preferred_element_type=F32) + lax.dot_general(
        stacked, low, dims, preferred_element_type=F32
    )


def full_dot(left, matrix, dims):
    left_high, left_low = high_low(left)
    high, low = high_low(matrix)
    total = lax.dot_general(left_high, high, dims, preferred_element_type=F32)
    total = total + lax.dot_general(left_low, high, dims, preferred_element_type=F32)
    return total + lax.dot_general(left_high, low, dims, preferred_element_type=F32)


def fold(rows):
    return rows[0:4] + rows[4:8]


def kernel(
    n_x, n_y, slots,
    vec_h, ord_h, near_h, bas_h, cl_h, tl_h, cn_h, tn_h, td_h, cu_h, pairs_h, pairs_s,
    out_ref,
    vec_v, ord_v, near_v, bas_v, cl_v, tl_v, cn_v, tn_v, td_v, cu_v, pairs_v,
    vs_v, onehot_v, ext, xs_v, nodex, mine, table, tbl2, prod, rs_send, rs_recv,
    far_node, near_y, y_v, g_v, w_high, w_low,
    small_sem, near_sem, cl_sem, cn_sem,
    halo_send, halo_recv, ag_send, ag_recv, rs_sent, rs_got,
):
    gi, gj = lax.axis_index("gx"), lax.axis_index("gy")
    devices = n_x * n_y
    me = gi * n_y + gj
    px, core, pz, py = lax.div(gi, 2), lax.rem(gi, 2), lax.div(gj, 4), lax.rem(gj, 4)
    others = []
    for dx, dy, dz, dc in OFFSETS:
        to_i = lax.rem(px + dx, 4) * 2 + lax.rem(core + dc, 2)
        to_j = lax.rem(pz + dz, 4) * 4 + lax.rem(py + dy, 4)
        others.append((to_i, to_j))

    small = [
        pltpu.make_async_copy(src, dst, small_sem.at[k])
        for k, (src, dst) in enumerate([
            (vec_h, vec_v), (ord_h, ord_v), (bas_h, bas_v), (tl_h, tl_v), (tn_h, tn_v),
            (td_h, td_v), (pairs_h, pairs_v), (cu_h, cu_v),
        ])
    ]
    for copy in small:
        copy.start()

    ext[...] = jnp.zeros_like(ext)

    barrier = pltpu.get_barrier_semaphore()
    for other in others:
        pl.semaphore_signal(barrier, inc=1, device_id=other, device_id_type=MESH)

    node_copy = pltpu.make_async_copy(cn_h, cn_v, cn_sem)

    def cl_copy(leaf):
        return pltpu.make_async_copy(cl_h.at[leaf], cl_v.at[leaf], cl_sem.at[leaf])

    def near_copy(leaf):
        return pltpu.make_async_copy(near_h.at[leaf], near_v.at[leaf], near_sem.at[leaf])

    def start_cl(u):
        for v in range(2):
            for s in range(2):
                for w in range(2):
                    cl_copy((2 * u + s) * 4 + 2 * v + w).start()

    for leaf in range(16):
        near_copy(leaf).start()
    node_copy.start()
    start_cl(0)

    def inside(dx, dy):
        ok = None
        for pos, step, count in ((gi, dx, n_x), (gj, dy, n_y)):
            if step == 0:
                continue
            here = pos + step < count if step > 0 else pos + step >= 0
            ok = here if ok is None else jnp.logical_and(ok, here)
        return ok

    small[0].wait()
    small[1].wait()
    vec = vec_v[...]
    vec_high = vec.astype(BF16).astype(F32)
    vec_low = vec - vec_high
    for kh in range(16):
        cols = slice(kh * 128, kh * 128 + 128)
        vs_v[kh * 8 : kh * 8 + 4, :] = vec_high[:, cols]
        vs_v[kh * 8 + 4 : kh * 8 + 8, :] = vec_low[:, cols]
    order = ord_v[...]
    order_low = jnp.bitwise_and(order, 127)
    order_high = lax.shift_right_logical(order, 7)
    sub = lax.broadcasted_iota(jnp.int32, (128, 128), 0)
    row_group = lax.shift_right_logical(sub, 3)
    vs = vs_v[...].astype(BF16)
    small[2].wait()
    for leaf in range(16):
        cols = slice(leaf * 128, leaf * 128 + 128)
        onehot = jnp.where(sub == order_low[:, cols], 1.0, 0.0).astype(BF16)
        onehot_v[:, cols] = onehot
        picked = lax.dot_general(vs, onehot, NN, preferred_element_type=F32)
        picked = jnp.where(row_group == order_high[:, cols], picked, 0.0)
        stacked = jnp.sum(picked.reshape(16, 8, 128), axis=0)
        up = fold(split_dot(stacked.astype(BF16), bas_v[leaf], NT))
        a, b = leaf // 4, leaf % 4
        ext[2 + a, 2 + b, 0:4, :] = fold(stacked)
        ext[2 + a, 2 + b, 4:8, 0:64] = up
        xs_v[1 + a, 1 + b] = stacked

    small[3].wait()
    small[4].wait()
    small[5].wait()
    up_device = jnp.zeros((8, 64), F32)
    for u in range(2):
        for v in range(2):
            node = jnp.zeros((8, 64), F32)
            for s in range(2):
                for w in range(2):
                    a, b = 2 * u + s, 2 * v + w
                    child = stack_split(ext[2 + a, 2 + b, 4:8, 0:64])
                    node = node + split_dot(child, tl_v[a * 4 + b], NN)
            node = fold(node)
            for p in range(2):
                for q in range(2):
                    ext[2 + 2 * p + u, 2 + 2 * q + v, 4:8, 64:128] = node
            up_device = up_device + split_dot(stack_split(node), tn_v[u * 2 + v], NN)
    up_device = fold(up_device)
    toward = fold(split_dot(stack_split(up_device), td_v[...], NN))
    mine[...] = jnp.concatenate([up_device, toward], 1)
    table[me] = mine[...]

    def near_sum(leaf, wanted):
        a, b = leaf // 4, leaf % 4
        rows, blocks = [], []
        for e in range(9):
            r, c = a + e // 3 - 1, b + e % 3 - 1
            if (0 <= r < 4 and 0 <= c < 4) == wanted:
                rows.append(xs_v[1 + r, 1 + c].astype(BF16))
                blocks.append(jnp.concatenate(high_low(near_v[leaf, e]), 0))
        if not rows:
            return jnp.zeros((8, 128), F32)
        both = lax.dot_general(
            jnp.concatenate(rows, 1), jnp.concatenate(blocks, 1), NT, preferred_element_type=F32
        )
        return both[:, 0:128] + both[:, 128:256]

    for leaf in range(16):
        near_copy(leaf).wait()
        near_y[leaf] = near_sum(leaf, True)

    pl.semaphore_wait(barrier, devices - 1)

    for to in others:
        pltpu.make_async_remote_copy(
            src_ref=mine, dst_ref=table.at[me], send_sem=ag_send, recv_sem=ag_recv,
            device_id=to, device_id_type=MESH).start()

    cut = {-1: (2, 2, 6), 0: (2, 4, 2), 1: (4, 2, 0)}

    def halo(index):
        dx, dy = DIRECTIONS[index]
        (r0, rn, rd), (c0, cn, cd) = cut[dx], cut[dy]
        return pltpu.make_async_remote_copy(
            src_ref=ext.at[r0 : r0 + rn, c0 : c0 + cn], dst_ref=ext.at[rd : rd + rn, cd : cd + cn],
            send_sem=halo_send.at[index], recv_sem=halo_recv.at[index],
            device_id=(gi + dx, gj + dy), device_id_type=MESH)

    for index, (dx, dy) in enumerate(DIRECTIONS):
        @pl.when(inside(dx, dy))
        def _(index=index):
            halo(index).start()

    start_cl(1)

    for u in range(2):
        for v in range(2):
            for s in range(2):
                for w in range(2):
                    leaf = (2 * u + s) * 4 + 2 * v + w
                    cols = slice(leaf * 128, leaf * 128 + 128)
                    step = full_dot(tl_v[leaf], bas_v[leaf], TN)
                    g_v[leaf] = step
                    step = full_dot(tn_v[u * 2 + v], step, TN)
                    high, low = high_low(step)
                    w_high[0:64, cols] = high
                    w_low[0:64, cols] = low
                    step = full_dot(td_v[...], step, TN)
                    high, low = high_low(step)
                    w_high[64:128, cols] = high
                    w_low[64:128, cols] = low

    for index, (dx, dy) in enumerate(DIRECTIONS):
        @pl.when(inside(dx, dy))
        def _(dx=dx, dy=dy):
            halo(DIRECTIONS.index((-dx, -dy))).wait_recv()

    for r in range(6):
        for c in range(6):
            if not (1 <= r <= 4 and 1 <= c <= 4):
                x = ext[r + 1, c + 1, 0:4, :]
                high = x.astype(BF16).astype(F32)
                xs_v[r, c, 0:4, :] = high
                xs_v[r, c, 4:8, :] = x - high
            tile_r, tile_c = (0, 2, 6)[r // 2] + r % 2, (0, 2, 6)[c // 2] + c % 2
            nodex[r, c, 0:4, :] = pltpu.roll(ext[tile_r, tile_c], 64, 1)[4:8]

    row8 = lax.broadcasted_iota(jnp.int32, (8, 64), 0)
    pick_row = [jnp.where(row8 == n, 1.0, 0.0).astype(BF16) for n in range(4)]

    def far_sum(blocks, source):
        acc = [jnp.zeros((64, 64), F32) for _ in range(4)]
        for g in range(27):
            block = blocks(g)
            for n in range(4):
                acc[n] = acc[n] + block * source(g, n)
        total = jnp.zeros((8, 64), F32)
        for n in range(4):
            for part in high_low(acc[n]):
                total = total + lax.dot_general(pick_row[n], part, NT, preferred_element_type=F32)
        return total[0:4]

    def far_leaf_group(u, v):
        node_rows = stack_split(far_node[2 * u + v, 0:4])
        for s in range(2):
            for w in range(2):
                layout = slots_of(s, w)
                leaf = (2 * u + s) * 4 + 2 * v + w
                cl_copy(leaf).wait()
                far = far_sum(
                    lambda g: cl_v[leaf, g],
                    lambda g, n: ext[2 * u + layout[g][0], 2 * v + layout[g][1], 4 + n : 5 + n, 0:64],
                )
                y = split_dot(stack_split(far), bas_v[leaf], NN)
                y = y + split_dot(node_rows, g_v[leaf], NN)
                near_y[leaf] = near_y[leaf] + y

    def far_node_group(box, s, w):
        layout = slots_of(s, w)
        far_node[box, 0:4] = far_sum(
            lambda g: cn_v[box, g],
            lambda g, n: nodex[layout[g][0], layout[g][1], n : n + 1, 0:64],
        )

    def loop(low, high, body):
        lax.fori_loop(low, high, lambda k, c: (body(k), c)[1], 0)

    node_copy.wait()
    for s in range(2):
        for w in range(2):
            far_node_group(2 * s + w, s, w)
    for leaf in range(16):
        if leaf not in (5, 6, 9, 10):
            near_y[leaf] = near_y[leaf] + near_sum(leaf, False)
    loop(0, 1, lambda v: far_leaf_group(0, v))

    most = pl.ds(0, devices - 1)

    def all_but_one(buffer, sent, got):
        return pltpu.make_async_remote_copy(
            src_ref=buffer.at[most], dst_ref=buffer.at[most], send_sem=sent, recv_sem=got,
            device_id=others[0], device_id_type=MESH)

    all_but_one(table, ag_send, ag_recv).wait_recv()

    full = table[...]
    groups = full.reshape(n_x // 2, 2, n_y // 2, 2, 4, 128).sum(axis=(1, 3)).reshape(devices // 4, 4, 128)
    high = full.astype(BF16).astype(F32)
    tbl2[0:devices, 0:4, :] = high
    tbl2[0:devices, 4:8, :] = full - high
    high = groups.astype(BF16).astype(F32)
    tbl2[devices:, 0:4, :] = pltpu.roll(high, 64, 2)
    tbl2[devices:, 4:8, :] = pltpu.roll(groups - high, 64, 2)

    small[6].wait()
    small[7].wait()
    for k in range(slots):
        stacked = tbl2[pairs_s[1, 0, k], :, 0:64].astype(BF16)
        prod[k * 8 : k * 8 + 4, 0:64] = fold(split_dot(stacked, cu_v[k], NT))

    target = pairs_v[0]
    row = lax.broadcasted_iota(jnp.int32, (devices, slots), 0)
    row_i, row_j = lax.div(row, n_y), lax.rem(row, n_y)
    parent_box = devices + lax.div(row_i, 2) * (n_y // 2) + lax.div(row_j, 2)
    pick_own = jnp.where(row == target, 1.0, 0.0).astype(BF16)
    pick_parent = jnp.where(parent_box == target, 1.0, 0.0).astype(BF16)
    for n in range(4):
        rows = prod[pl.ds(n, 40, stride=8), :][0:slots, 0:64]
        sums = []
        for pick in (pick_own, pick_parent):
            part = 0.0
            for piece in high_low(rows):
                part = part + lax.dot_general(pick, piece, NN, preferred_element_type=F32)
            sums.append(part)
        both = jnp.concatenate(sums, 1)
        rs_send[:, n : n + 1, :] = both.reshape(devices, 1, 128)

    for to_i, to_j in others:
        pltpu.make_async_remote_copy(
            src_ref=rs_send.at[to_i * n_y + to_j], dst_ref=rs_recv.at[me],
            send_sem=rs_sent, recv_sem=rs_got,
            device_id=(to_i, to_j), device_id_type=MESH).start()
    rs_recv[me] = rs_send[me]

    loop(1, 2, lambda v: far_leaf_group(0, v))
    loop(0, 2, lambda v: far_leaf_group(1, v))

    all_but_one(rs_recv, rs_sent, rs_got).wait_recv()
    sums = stack_split(jnp.sum(rs_recv[...], axis=0))

    down = lax.dot_general(sums, w_high[...], NN, preferred_element_type=F32)
    down = down + lax.dot_general(sums, w_low[...], NN, preferred_element_type=F32)
    for leaf in range(16):
        cols = slice(leaf * 128, leaf * 128 + 128)
        y_v[:, cols] = stack_split(fold(near_y[leaf] + down[:, cols])).astype(F32)

    total = jnp.zeros((128, 128), F32)
    for leaf in range(16):
        cols = slice(leaf * 128, leaf * 128 + 128)
        y = y_v[:, cols]
        spread = jnp.broadcast_to(y[None], (16, 8, 128)).reshape(128, 128)
        spread = jnp.where(row_group == order_high[:, cols], spread, 0.0).astype(BF16)
        total = total + lax.dot_general(spread, onehot_v[:, cols], NT, preferred_element_type=F32)
    for kh in range(16):
        out_ref[:, kh * 128 : kh * 128 + 128] = fold(total[kh * 8 : kh * 8 + 8])

    all_but_one(table, ag_send, ag_recv).wait_send()
    all_but_one(rs_send, rs_sent, rs_got).wait_send()
    for index, (dx, dy) in enumerate(DIRECTIONS):
        @pl.when(inside(dx, dy))
        def _(index=index):
            halo(index).wait_send()


def on_device(
    n_x, n_y,
    vectors, cluster_order, near_blocks, leaf_basis, couple_leaf, transfer_leaf,
    couple_node, transfer_node, transfer_device, couple_upper, pair_list,
):
    slots = couple_upper.shape[1]
    devices = n_x * n_y
    near = near_blocks.transpose(0, 1, 3, 2, 4).reshape(16, 9, 128, 128)
    basis = leaf_basis.transpose(0, 1, 3, 2).reshape(16, 64, 128)
    cl = couple_leaf.transpose(0, 1, 3, 2, 4).reshape(16, 27, 64, 64)
    cn = couple_node.transpose(0, 1, 3, 2, 4).reshape(4, 27, 64, 64)
    tl = transfer_leaf.reshape(16, 64, 64)
    tn = transfer_node.reshape(4, 64, 64)
    td = transfer_device.reshape(64, 64)
    cu = couple_upper.reshape(slots, 64, 64)
    dma = pltpu.SemaphoreType.DMA
    any_spec = pl.BlockSpec(memory_space=pl.ANY)
    return pl.pallas_call(
        functools.partial(kernel, n_x, n_y, slots),
        out_shape=jax.ShapeDtypeStruct((4, 2048), F32),
        in_specs=[any_spec] * 11 + [pl.BlockSpec(memory_space=pltpu.SMEM)],
        out_specs=pl.BlockSpec(memory_space=pltpu.VMEM),
        scratch_shapes=[
            pltpu.VMEM((4, 2048), F32),
            pltpu.VMEM((1, 2048), jnp.int32),
            pltpu.VMEM((16, 9, 128, 128), F32),
            pltpu.VMEM((16, 64, 128), F32),
            pltpu.VMEM((16, 27, 64, 64), F32),
            pltpu.VMEM((16, 64, 64), F32),
            pltpu.VMEM((4, 27, 64, 64), F32),
            pltpu.VMEM((4, 64, 64), F32),
            pltpu.VMEM((64, 64), F32),
            pltpu.VMEM((slots, 64, 64), F32),
            pltpu.VMEM((2, 1, slots), jnp.int32),
            pltpu.VMEM((128, 128), F32),
            pltpu.VMEM((128, 2048), BF16),
            pltpu.VMEM((8, 8, 8, 128), F32),
            pltpu.VMEM((6, 6, 8, 128), F32),
            pltpu.VMEM((6, 6, 8, 128), F32),
            pltpu.VMEM((4, 128), F32),
            pltpu.VMEM((devices, 4, 128), F32),
            pltpu.VMEM((devices + devices // 4, 8, 128), F32),
            pltpu.VMEM((320, 128), F32),
            pltpu.VMEM((devices, 4, 128), F32),
            pltpu.VMEM((devices, 4, 128), F32),
            pltpu.VMEM((4, 8, 64), F32),
            pltpu.VMEM((16, 8, 128), F32),
            pltpu.VMEM((8, 2048), F32),
            pltpu.VMEM((16, 64, 128), F32),
            pltpu.VMEM((128, 2048), BF16),
            pltpu.VMEM((128, 2048), BF16),
            dma((8,)), dma((16,)), dma((16,)), dma(()),
            dma((8,)), dma((8,)), dma(()), dma(()), dma(()), dma(()),
        ],
        compiler_params=pltpu.CompilerParams(
            collective_id=0, has_side_effects=True, vmem_limit_bytes=56 * 1024 * 1024
        ),
    )(vectors, cluster_order, near, basis, cl, tl, cn, tn, td, cu, pair_list, pair_list)


def solution(mesh):
    in_specs = (
        P(None, ("gx", "gy")),
        P(("gx", "gy"), None),
        P("gx", "gy", None, None, None),
        P("gx", "gy", None, None),
        P("gx", "gy", None, None, None),
        P("gx", "gy", None, None),
        P("gx", "gy", None, None, None),
        P("gx", "gy", None, None),
        P("gx", "gy", None, None),
        P(("gx", "gy"), None, None, None),
        P(None, ("gx", "gy"), None),
    )
    out_specs = P(None, ("gx", "gy"))
    return jax.shard_map(
        functools.partial(on_device, mesh.shape["gx"], mesh.shape["gy"]),
        mesh=mesh, in_specs=in_specs, out_specs=out_specs, check_vma=False,
    )
```

time: 41.7 us -> 37.4 us (0.90)
  Pallas kernels: 39.9 us -> 35.8 us
    pallas_call x1, Pallas kernels: 39.9 us -> 35.8 us  [on_device(): pl.pallas_call(functools.partial(kernel, n_x, n_y, slots), out_shape=jax....]
where the time goes in v1:
time: 37.4 us; the launch traced here: 37.2 us
  Pallas kernels  35.8 us (96%)
  local copies, waits for them, and re-layouts  1.38 us (4%)
    pallas_call x1, Pallas kernels, on_device(): pl.pallas_call(functools.partial(kernel, n_x, n_y, slots), out_shape=jax....  35.8 us
    unnamed x1, local copies, waits for them, and re-layouts  1.38 us

profile of v1, /device:TPU:1, one launch (start us, length us, event | category | flops | bytes accessed | tf_op | source)
XLA Modules:
  0.0 37.2 jit_solution(5319081276903617065)
XLA Ops:
  0.0 35.8 %shard_map.109 = f32[4,2048]{1,0:T(4,128)} custom-call(f32[4,2048]{1,0:T(4,128)} %vec_h.1, s32[1,2048]{1,0:T(1,128)} %ord_h.1, f32[16,9,128,128]{3,2,1,0:T(8,128)} %bitcast.17, f32[16,64,128]{2,1,0:T(8,128)} %bitcast.20, f32[16,27,64,64]{3,2,1,0:T(8,128)} %bitcast.16, f32[16,64,64]{2,1,0:T(8,128)} %bitcast.21, f32[4,27,64,64]{3,2,1,0:T(8,128)} %bitcast.18, ...), custom_call_target="tpu_custom_call" | custom-call | tf_op jit(solution)/shard_map/pallas_call | solution.py:405
  35.8 1.4 %copy.13 = f32[4,2048]{1,0:T(4,128)} copy(f32[4,2048]{1,0:T(4,128)} %shard_map.109) | data formatting | bytes 65536

commit v2 on v1

--- a/solution.py
+++ b/solution.py
@@ -73,8 +73,8 @@
     vec_h, ord_h, near_h, bas_h, cl_h, tl_h, cn_h, tn_h, td_h, cu_h, pairs_h, pairs_s,
     out_ref,
     vec_v, ord_v, near_v, bas_v, cl_v, tl_v, cn_v, tn_v, td_v, cu_v, pairs_v,
-    vs_v, onehot_v, ext, xs_v, nodex, mine, table, tbl2, prod, rs_send, rs_recv,
-    far_node, near_y, y_v, g_v, w_high, w_low,
+    vs_v, onehot_v, ext, xs_v, leaf_row, leaf_col, node_row, node_col, mine, table, tbl2, prod, rs_send, rs_recv,
+    raw_far, near_y, y_v, g_v, w_high, w_low,
     small_sem, near_sem, cl_sem, cn_sem,
     halo_send, halo_recv, ag_send, ag_recv, rs_sent, rs_got,
 ):
@@ -122,6 +122,7 @@
         near_copy(leaf).start()
     node_copy.start()
     start_cl(0)
+    start_cl(1)
 
     def inside(dx, dy):
         ok = None
@@ -198,10 +199,6 @@
         )
         return both[:, 0:128] + both[:, 128:256]
 
-    for leaf in range(16):
-        near_copy(leaf).wait()
-        near_y[leaf] = near_sum(leaf, True)
-
     pl.semaphore_wait(barrier, devices - 1)
 
     for to in others:
@@ -224,24 +221,32 @@
         def _(index=index):
             halo(index).start()
 
-    start_cl(1)
+    for leaf in range(16):
+        near_copy(leaf).wait()
+    for leaf in range(16):
+        near_y[leaf] = near_sum(leaf, True)
+
+    small[6].wait()
+    target = pairs_v[0]
+    row = lax.broadcasted_iota(jnp.int32, (devices, slots), 0)
+    row_i, row_j = lax.div(row, n_y), lax.rem(row, n_y)
+    parent_box = devices + lax.div(row_i, 2) * (n_y // 2) + lax.div(row_j, 2)
+    pick_own = jnp.where(row == target, 1.0, 0.0).astype(BF16)
+    pick_parent = jnp.where(parent_box == target, 1.0, 0.0).astype(BF16)
 
     for u in range(2):
         for v in range(2):
-            for s in range(2):
-                for w in range(2):
-                    leaf = (2 * u + s) * 4 + 2 * v + w
-                    cols = slice(leaf * 128, leaf * 128 + 128)
-                    step = full_dot(tl_v[leaf], bas_v[leaf], TN)
-                    g_v[leaf] = step
-                    step = full_dot(tn_v[u * 2 + v], step, TN)
-                    high, low = high_low(step)
-                    w_high[0:64, cols] = high
-                    w_low[0:64, cols] = low
-                    step = full_dot(td_v[...], step, TN)
-                    high, low = high_low(step)
-                    w_high[64:128, cols] = high
-                    w_low[64:128, cols] = low
+            family = [(2 * u + s) * 4 + 2 * v + w for s in range(2) for w in range(2)]
+            steps = [full_dot(tl_v[leaf], bas_v[leaf], TN) for leaf in family]
+            for leaf, step in zip(family, steps):
+                g_v[leaf] = step
+            down = full_dot(tn_v[u * 2 + v], jnp.concatenate(steps, 1), TN)
+            both = jnp.concatenate([down, full_dot(td_v[...], down, TN)], 0)
+            high, low = high_low(both)
+            for k, leaf in enumerate(family):
+                cols = slice(leaf * 128, leaf * 128 + 128)
+                w_high[:, cols] = high[:, k * 128 : k * 128 + 128]
+                w_low[:, cols] = low[:, k * 128 : k * 128 + 128]
 
     for index, (dx, dy) in enumerate(DIRECTIONS):
         @pl.when(inside(dx, dy))
@@ -255,57 +260,84 @@
                 high = x.astype(BF16).astype(F32)
                 xs_v[r, c, 0:4, :] = high
                 xs_v[r, c, 4:8, :] = x - high
-            tile_r, tile_c = (0, 2, 6)[r // 2] + r % 2, (0, 2, 6)[c // 2] + c % 2
-            nodex[r, c, 0:4, :] = pltpu.roll(ext[tile_r, tile_c], 64, 1)[4:8]
-
-    row8 = lax.broadcasted_iota(jnp.int32, (8, 64), 0)
-    pick_row = [jnp.where(row8 == n, 1.0, 0.0).astype(BF16) for n in range(4)]
-
-    def far_sum(blocks, source):
-        acc = [jnp.zeros((64, 64), F32) for _ in range(4)]
-        for g in range(27):
-            block = blocks(g)
+
+    lane = lax.broadcasted_iota(jnp.int32, (8, 128), 1)
+
+    def side_by_side(left, right):
+        return jnp.where(lane < 64, left, right)
+
+    node_at = (0, 1, 2, 3, 6, 7)
+    for r in range(8):
+        for c in range(8):
+            swapped = pltpu.roll(ext[r, c], 64, 1)
+            if c > 0:
+                leaf_row[r, c - 1] = side_by_side(ext[r, c - 1], swapped)
+            if r > 0:
+                leaf_col[r - 1, c] = side_by_side(ext[r - 1, c], swapped)
+    for r in range(6):
+        for c in range(6):
+            here = ext[node_at[r], node_at[c]]
+            swapped = pltpu.roll(here, 64, 1)
+            if c < 5:
+                node_row[r, c] = side_by_side(swapped, ext[node_at[r], node_at[c + 1]])
+            if r < 5:
+                node_col[r, c] = side_by_side(swapped, ext[node_at[r + 1], node_at[c]])
+
+    row8 = lax.broadcasted_iota(jnp.int32, (8, 512), 0)
+    group8 = lax.shift_right_logical(lax.broadcasted_iota(jnp.int32, (8, 512), 1), 7)
+    pick_row = jnp.where(row8 == group8, 1.0, 0.0).astype(BF16)
+
+    def far_sum(s, w, blocks, row_pair, column_pair):
+        layout = slots_of(s, w)
+        acc = [jnp.zeros((64, 128), F32) for _ in range(4)]
+
+        def add(left, right, source):
+            pair = jnp.concatenate([blocks(left), jnp.zeros((64, 64), F32) if right is None else blocks(right)], 1)
             for n in range(4):
-                acc[n] = acc[n] + block * source(g, n)
-        total = jnp.zeros((8, 64), F32)
-        for n in range(4):
-            for part in high_low(acc[n]):
-                total = total + lax.dot_general(pick_row[n], part, NT, preferred_element_type=F32)
-        return total[0:4]
-
-    def far_leaf_group(u, v):
-        node_rows = stack_split(far_node[2 * u + v, 0:4])
+                acc[n] = acc[n] + pair * source(n)
+
+        lone = 0 if w == 0 else 5
+        pairs_in_row = ((4, 5),) if w == 0 else ((0, 1),)
+        for i in range(6):
+            for j, j2 in pairs_in_row if s + 1 <= i <= s + 3 else ((0, 1), (2, 3), (4, 5)):
+                add(layout.index((i, j)), layout.index((i, j2)), lambda n: row_pair(i, j, n))
+        add(layout.index((s + 1, lone)), layout.index((s + 2, lone)), lambda n: column_pair(s + 1, lone, n))
+        add(layout.index((s + 3, lone)), None, lambda n: column_pair(s + 3, lone, n))
+        return acc
+
+    def over_q(acc):
+        parts = jnp.concatenate(high_low(jnp.concatenate(acc, 1)), 0)
+        both = lax.dot_general(pick_row, parts, NT, preferred_element_type=F32)
+        return both[0:4, 0:64] + both[0:4, 64:128]
+
+    def far_leaf_sums(u, v):
         for s in range(2):
             for w in range(2):
-                layout = slots_of(s, w)
                 leaf = (2 * u + s) * 4 + 2 * v + w
-                cl_copy(leaf).wait()
-                far = far_sum(
-                    lambda g: cl_v[leaf, g],
-                    lambda g, n: ext[2 * u + layout[g][0], 2 * v + layout[g][1], 4 + n : 5 + n, 0:64],
+                acc = far_sum(
+                    s, w, lambda g: cl_v[leaf, g],
+                    lambda i, j, n: leaf_row[2 * u + i, 2 * v + j, 4 + n : 5 + n, :],
+                    lambda i, j, n: leaf_col[2 * u + i, 2 * v + j, 4 + n : 5 + n, :],
                 )
-                y = split_dot(stack_split(far), bas_v[leaf], NN)
-                y = y + split_dot(node_rows, g_v[leaf], NN)
-                near_y[leaf] = near_y[leaf] + y
-
-    def far_node_group(box, s, w):
-        layout = slots_of(s, w)
-        far_node[box, 0:4] = far_sum(
-            lambda g: cn_v[box, g],
-            lambda g, n: nodex[layout[g][0], layout[g][1], n : n + 1, 0:64],
-        )
-
-    def loop(low, high, body):
-        lax.fori_loop(low, high, lambda k, c: (body(k), c)[1], 0)
-
-    node_copy.wait()
-    for s in range(2):
-        for w in range(2):
-            far_node_group(2 * s + w, s, w)
+                for n in range(4):
+                    raw_far[leaf, n] = acc[n]
+
+    def far_node_sums(box, s, w):
+        return over_q(far_sum(
+            s, w, lambda g: cn_v[box, g],
+            lambda i, j, n: node_row[i, j, 4 + n : 5 + n, :],
+            lambda i, j, n: node_col[i, j, 4 + n : 5 + n, :],
+        ))
+
+    def leaf_part(leaf, node_sum):
+        far = over_q([raw_far[leaf, n] for n in range(4)])
+        rows = stack_split(jnp.concatenate([far, node_sum], 1))
+        down = jnp.concatenate([bas_v[leaf], g_v[leaf]], 0)
+        near_y[leaf] = near_y[leaf] + split_dot(rows, down, NN)
+
     for leaf in range(16):
         if leaf not in (5, 6, 9, 10):
             near_y[leaf] = near_y[leaf] + near_sum(leaf, False)
-    loop(0, 1, lambda v: far_leaf_group(0, v))
 
     most = pl.ds(0, devices - 1)
 
@@ -325,18 +357,11 @@
     tbl2[devices:, 0:4, :] = pltpu.roll(high, 64, 2)
     tbl2[devices:, 4:8, :] = pltpu.roll(groups - high, 64, 2)
 
-    small[6].wait()
     small[7].wait()
     for k in range(slots):
         stacked = tbl2[pairs_s[1, 0, k], :, 0:64].astype(BF16)
         prod[k * 8 : k * 8 + 4, 0:64] = fold(split_dot(stacked, cu_v[k], NT))
 
-    target = pairs_v[0]
-    row = lax.broadcasted_iota(jnp.int32, (devices, slots), 0)
-    row_i, row_j = lax.div(row, n_y), lax.rem(row, n_y)
-    parent_box = devices + lax.div(row_i, 2) * (n_y // 2) + lax.div(row_j, 2)
-    pick_own = jnp.where(row == target, 1.0, 0.0).astype(BF16)
-    pick_parent = jnp.where(parent_box == target, 1.0, 0.0).astype(BF16)
     for n in range(4):
         rows = prod[pl.ds(n, 40, stride=8), :][0:slots, 0:64]
         sums = []
@@ -355,8 +380,16 @@
             device_id=(to_i, to_j), device_id_type=MESH).start()
     rs_recv[me] = rs_send[me]
 
-    loop(1, 2, lambda v: far_leaf_group(0, v))
-    loop(0, 2, lambda v: far_leaf_group(1, v))
+    node_copy.wait()
+    for leaf in range(16):
+        cl_copy(leaf).wait()
+    lax.fori_loop(0, 4, lambda k, c: (far_leaf_sums(lax.div(k, 2), lax.rem(k, 2)), c)[1], 0)
+    for u in range(2):
+        for v in range(2):
+            node_sum = far_node_sums(2 * u + v, u, v)
+            for s in range(2):
+                for w in range(2):
+                    leaf_part((2 * u + s) * 4 + 2 * v + w, node_sum)
 
     all_but_one(rs_recv, rs_sent, rs_got).wait_recv()
     sums = stack_split(jnp.sum(rs_recv[...], axis=0))
@@ -423,14 +456,17 @@
             pltpu.VMEM((128, 2048), BF16),
             pltpu.VMEM((8, 8, 8, 128), F32),
             pltpu.VMEM((6, 6, 8, 128), F32),
-            pltpu.VMEM((6, 6, 8, 128), F32),
+            pltpu.VMEM((8, 7, 8, 128), F32),
+            pltpu.VMEM((7, 8, 8, 128), F32),
+            pltpu.VMEM((6, 5, 8, 128), F32),
+            pltpu.VMEM((5, 6, 8, 128), F32),
             pltpu.VMEM((4, 128), F32),
             pltpu.VMEM((devices, 4, 128), F32),
             pltpu.VMEM((devices + devices // 4, 8, 128), F32),
             pltpu.VMEM((320, 128), F32),
             pltpu.VMEM((devices, 4, 128), F32),
             pltpu.VMEM((devices, 4, 128), F32),
-            pltpu.VMEM((4, 8, 64), F32),
+            pltpu.VMEM((16, 4, 64, 128), F32),
             pltpu.VMEM((16, 8, 128), F32),
             pltpu.VMEM((8, 2048), F32),
             pltpu.VMEM((16, 64, 128), F32),

time: 37.4 us -> 32 us (0.86)
  Pallas kernels: 35.8 us -> 30.4 us
    pallas_call x1, Pallas kernels: 35.8 us -> 30.4 us  [on_device(): pl.pallas_call(functools.partial(kernel, n_x, n_y, slots), out_shape=jax....]
where the time goes in v2:
time: 32 us; the launch traced here: 31.8 us
  Pallas kernels  30.4 us (95%)
  local copies, waits for them, and re-layouts  1.38 us (4%)
    pallas_call x1, Pallas kernels, on_device(): pl.pallas_call(functools.partial(kernel, n_x, n_y, slots), out_shape=jax....  30.4 us
    unnamed x1, local copies, waits for them, and re-layouts  1.38 us

profile of v2, /device:TPU:1, one launch (start us, length us, event | category | flops | bytes accessed | tf_op | source)
XLA Modules:
  0.0 31.8 jit_solution(1700352725839194884)
XLA Ops:
  0.0 30.4 %shard_map.109 = f32[4,2048]{1,0:T(4,128)} custom-call(f32[4,2048]{1,0:T(4,128)} %vec_h.1, s32[1,2048]{1,0:T(1,128)} %ord_h.1, f32[16,9,128,128]{3,2,1,0:T(8,128)} %bitcast.17, f32[16,64,128]{2,1,0:T(8,128)} %bitcast.20, f32[16,27,64,64]{3,2,1,0:T(8,128)} %bitcast.16, f32[16,64,64]{2,1,0:T(8,128)} %bitcast.21, f32[4,27,64,64]{3,2,1,0:T(8,128)} %bitcast.18, ...), custom_call_target="tpu_custom_call" | custom-call | tf_op jit(solution)/shard_map/pallas_call | solution.py:438
  30.4 1.4 %copy.13 = f32[4,2048]{1,0:T(4,128)} copy(f32[4,2048]{1,0:T(4,128)} %shard_map.109) | data formatting | bytes 65536

commit v3 on v2

--- a/solution.py
+++ b/solution.py
@@ -83,10 +83,10 @@
     me = gi * n_y + gj
     px, core, pz, py = lax.div(gi, 2), lax.rem(gi, 2), lax.div(gj, 4), lax.rem(gj, 4)
     others = []
+    along_x = [[lax.rem(px + d, 4) * 2 + lax.rem(core + c, 2) for c in range(2)] for d in range(4)]
+    along_zy = [[lax.rem(pz + z, 4) * 4 + lax.rem(py + y, 4) for y in range(4)] for z in range(4)]
     for dx, dy, dz, dc in OFFSETS:
-        to_i = lax.rem(px + dx, 4) * 2 + lax.rem(core + dc, 2)
-        to_j = lax.rem(pz + dz, 4) * 4 + lax.rem(py + dy, 4)
-        others.append((to_i, to_j))
+        others.append((along_x[dx][dc], along_zy[dz][dy]))
 
     small = [
         pltpu.make_async_copy(src, dst, small_sem.at[k])
@@ -229,8 +229,10 @@
     small[6].wait()
     target = pairs_v[0]
     row = lax.broadcasted_iota(jnp.int32, (devices, slots), 0)
-    row_i, row_j = lax.div(row, n_y), lax.rem(row, n_y)
-    parent_box = devices + lax.div(row_i, 2) * (n_y // 2) + lax.div(row_j, 2)
+    bits = n_y.bit_length() - 1
+    half_i = lax.shift_right_logical(row, bits + 1)
+    half_j = lax.shift_right_logical(jnp.bitwise_and(row, n_y - 1), 1)
+    parent_box = devices + half_i * (n_y // 2) + half_j
     pick_own = jnp.where(row == target, 1.0, 0.0).astype(BF16)
     pick_parent = jnp.where(parent_box == target, 1.0, 0.0).astype(BF16)
 
@@ -247,6 +249,47 @@
                 cols = slice(leaf * 128, leaf * 128 + 128)
                 w_high[:, cols] = high[:, k * 128 : k * 128 + 128]
                 w_low[:, cols] = low[:, k * 128 : k * 128 + 128]
+
+    most = pl.ds(0, devices - 1)
+
+    def all_but_one(buffer, sent, got):
+        return pltpu.make_async_remote_copy(
+            src_ref=buffer.at[most], dst_ref=buffer.at[most], send_sem=sent, recv_sem=got,
+            device_id=others[0], device_id_type=MESH)
+
+    all_but_one(table, ag_send, ag_recv).wait_recv()
+
+    full = table[...]
+    groups = full.reshape(n_x // 2, 2, n_y // 2, 2, 4, 128).sum(axis=(1, 3)).reshape(devices // 4, 4, 128)
+    high = full.astype(BF16).astype(F32)
+    tbl2[0:devices, 0:4, :] = high
+    tbl2[0:devices, 4:8, :] = full - high
+    high = groups.astype(BF16).astype(F32)
+    tbl2[devices:, 0:4, :] = pltpu.roll(high, 64, 2)
+    tbl2[devices:, 4:8, :] = pltpu.roll(groups - high, 64, 2)
+
+    small[7].wait()
+    for k in range(slots):
+        stacked = tbl2[pairs_s[1, 0, k], :, 0:64].astype(BF16)
+        prod[k * 8 : k * 8 + 4, 0:64] = fold(split_dot(stacked, cu_v[k], NT))
+
+    for n in range(4):
+        rows = prod[pl.ds(n, 40, stride=8), :][0:slots, 0:64]
+        sums = []
+        for pick in (pick_own, pick_parent):
+            part = 0.0
+            for piece in high_low(rows):
+                part = part + lax.dot_general(pick, piece, NN, preferred_element_type=F32)
+            sums.append(part)
+        both = jnp.concatenate(sums, 1)
+        rs_send[:, n : n + 1, :] = both.reshape(devices, 1, 128)
+
+    for to_i, to_j in others:
+        pltpu.make_async_remote_copy(
+            src_ref=rs_send.at[to_i * n_y + to_j], dst_ref=rs_recv.at[me],
+            send_sem=rs_sent, recv_sem=rs_got,
+            device_id=(to_i, to_j), device_id_type=MESH).start()
+    rs_recv[me] = rs_send[me]
 
     for index, (dx, dy) in enumerate(DIRECTIONS):
         @pl.when(inside(dx, dy))
@@ -338,47 +381,6 @@
     for leaf in range(16):
         if leaf not in (5, 6, 9, 10):
             near_y[leaf] = near_y[leaf] + near_sum(leaf, False)
-
-    most = pl.ds(0, devices - 1)
-
-    def all_but_one(buffer, sent, got):
-        return pltpu.make_async_remote_copy(
-            src_ref=buffer.at[most], dst_ref=buffer.at[most], send_sem=sent, recv_sem=got,
-            device_id=others[0], device_id_type=MESH)
-
-    all_but_one(table, ag_send, ag_recv).wait_recv()
-
-    full = table[...]
-    groups = full.reshape(n_x // 2, 2, n_y // 2, 2, 4, 128).sum(axis=(1, 3)).reshape(devices // 4, 4, 128)
-    high = full.astype(BF16).astype(F32)
-    tbl2[0:devices, 0:4, :] = high
-    tbl2[0:devices, 4:8, :] = full - high
-    high = groups.astype(BF16).astype(F32)
-    tbl2[devices:, 0:4, :] = pltpu.roll(high, 64, 2)
-    tbl2[devices:, 4:8, :] = pltpu.roll(groups - high, 64, 2)
-
-    small[7].wait()
-    for k in range(slots):
-        stacked = tbl2[pairs_s[1, 0, k], :, 0:64].astype(BF16)
-        prod[k * 8 : k * 8 + 4, 0:64] = fold(split_dot(stacked, cu_v[k], NT))
-
-    for n in range(4):
-        rows = prod[pl.ds(n, 40, stride=8), :][0:slots, 0:64]
-        sums = []
-        for pick in (pick_own, pick_parent):
-            part = 0.0
-            for piece in high_low(rows):
-                part = part + lax.dot_general(pick, piece, NN, preferred_element_type=F32)
-            sums.append(part)
-        both = jnp.concatenate(sums, 1)
-        rs_send[:, n : n + 1, :] = both.reshape(devices, 1, 128)
-
-    for to_i, to_j in others:
-        pltpu.make_async_remote_copy(
-            src_ref=rs_send.at[to_i * n_y + to_j], dst_ref=rs_recv.at[me],
-            send_sem=rs_sent, recv_sem=rs_got,
-            device_id=(to_i, to_j), device_id_type=MESH).start()
-    rs_recv[me] = rs_send[me]
 
     node_copy.wait()
     for leaf in range(16):

time: 32 us -> 31 us (0.969)
  Pallas kernels: 30.4 us -> 29.4 us
    pallas_call x1, Pallas kernels: 30.4 us -> 29.4 us  [on_device(): pl.pallas_call(functools.partial(kernel, n_x, n_y, slots), out_shape=jax....]
where the time goes in v3:
time: 31 us; the launch traced here: 30.8 us
  Pallas kernels  29.4 us (95%)
  local copies, waits for them, and re-layouts  1.38 us (4%)
    pallas_call x1, Pallas kernels, on_device(): pl.pallas_call(functools.partial(kernel, n_x, n_y, slots), out_shape=jax....  29.4 us
    unnamed x1, local copies, waits for them, and re-layouts  1.38 us

profile of v3, /device:TPU:1, one launch (start us, length us, event | category | flops | bytes accessed | tf_op | source)
XLA Modules:
  0.0 30.8 jit_solution(1291877373607395957)
XLA Ops:
  0.0 29.4 %shard_map.109 = f32[4,2048]{1,0:T(4,128)} custom-call(f32[4,2048]{1,0:T(4,128)} %vec_h.1, s32[1,2048]{1,0:T(1,128)} %ord_h.1, f32[16,9,128,128]{3,2,1,0:T(8,128)} %bitcast.17, f32[16,64,128]{2,1,0:T(8,128)} %bitcast.20, f32[16,27,64,64]{3,2,1,0:T(8,128)} %bitcast.16, f32[16,64,64]{2,1,0:T(8,128)} %bitcast.21, f32[4,27,64,64]{3,2,1,0:T(8,128)} %bitcast.18, ...), custom_call_target="tpu_custom_call" | custom-call | tf_op jit(solution)/shard_map/pallas_call | solution.py:440
  29.5 1.4 %copy.13 = f32[4,2048]{1,0:T(4,128)} copy(f32[4,2048]{1,0:T(4,128)} %shard_map.109) | data formatting | bytes 65536
